TPU v7x, 32 devices: a whole 2x2x4 slice. The times are simulated.
32 devices in a mesh: dp: 4 (over z), seq: 8 (over y, x, core).
Axes of the slice: x: 2, y: 2, z: 4, core: 2. Of those that a mesh axis runs over, the one named last changes fastest.
Arguments:
- queries: bfloat16 [12288, 2048], P(('dp', 'seq')), parts along dimension 0, may hold values from -6 to 6
- keys_in: bfloat16 [12288, 2048], P(('dp', 'seq')), parts along dimension 0, may hold values from -6 to 6
- values: bfloat16 [12288, 2048], P(('dp', 'seq')), parts along dimension 0, may hold values from -6 to 6
- stream: bfloat16 [12288, 2048], P(('dp', 'seq')), parts along dimension 0, may hold values from -6 to 6
- log_decay: float32 [12288, 16], P(('dp', 'seq')), parts along dimension 0, may hold values from -1 to 0
- token_index: int32 [32, 768], P('dp', 'seq'), parts along dimension 0, may hold values from 0 to 3071, as said below
- route_weight: float32 [32, 768], P('dp', 'seq'), parts along dimension 0, may hold values from 0.2 to 1
- moe_gain: float32 [2048], replicated, may hold values from 0.25 to 1.75
- out_weight: bfloat16 [2048, 2048], P('seq'), may hold values from -0.125 to 0.125
- gate_weight: bfloat16 [8, 2048, 1408], P('seq'), may hold values from -0.125 to 0.125
- up_weight: bfloat16 [8, 2048, 1408], P('seq'), may hold values from -0.125 to 0.125
- down_weight: bfloat16 [8, 1408, 2048], P('seq'), may hold values from -0.15625 to 0.15625
Outputs:
- mixed: bfloat16 [12288, 2048], P(('dp', 'seq')), parts along dimension 0
There are 4 independent parts, one for each index of `dp`. A program takes and returns all parts, laid end to end along the dimension named above; an argument that names none is the same for every part. Nothing has to cross between parts.
Inputs may be any that keep to these rules, and one draw needn't show every extreme that they name: `token_index`: for each expert and each j, positions j * 96 to (j + 1) * 96 - 1 of its row hold 96 different tokens of the j-th block of 384 tokens, in ascending order.
All inputs are finite; a program needn't handle non-finite values.
Results may differ from a plain program's by a relative error of at most 0.014.
Values may be sent and summed in bfloat16 or wider, within the bound.
A program may use at most 192 MiB of HBM per device.

v0:
```python
import jax
import jax.numpy as jnp
from jax import lax
from jax.sharding import PartitionSpec as P


def carried_in(array, axis, combine, identity):
    count, index = (lax.axis_size(axis), lax.axis_index(axis))
    everything = jax.tree.map(
        lambda part, kind: lax.all_gather(part.astype(kind), axis),
        array,
        (jnp.bfloat16, jnp.bfloat16),
    )
    start = jax.tree.map(
        lambda part, zero: jnp.broadcast_to(jnp.asarray(zero, part.dtype), part.shape),
        array,
        identity,
    )

    def turn(k, before):
        reached = k < index
        new = combine(
            before, jax.tree.map(lambda part, own: part[k].astype(own.dtype), everything, array)
        )
        return jax.tree.map(lambda a, b: jnp.where(reached, a, b), new, before)

    return lax.fori_loop(0, count, turn, start)


def shards(
    queries,
    keys_in,
    values,
    stream,
    log_decay,
    token_index,
    route_weight,
    moe_gain,
    out_weight,
    gate_weight,
    up_weight,
    down_weight,
):
    length, model_width = queries.shape
    head_count = log_decay.shape[1]
    head_size = model_width // head_count
    scaling = head_size ** (-0.5)
    device = lax.axis_index("seq")
    query_heads = queries.reshape(length, head_count, head_size)
    key_heads = keys_in.reshape(length, head_count, head_size)
    value_heads = values.reshape(length, head_count, head_size)
    running = jnp.cumsum(log_decay, axis=0)
    ending = running[-1]
    shrink = jnp.exp(ending[None, :] - running)
    key_scaled = (key_heads.astype(jnp.float32) * shrink[:, :, None]).astype(jnp.bfloat16)
    local_state = jnp.einsum(
        "shd,she->hde", key_scaled, value_heads, preferred_element_type=jnp.float32
    )
    zero_state = jnp.zeros_like(local_state)

    def combine(earlier, latter):
        return (earlier[0] * jnp.exp(latter[1])[:, None, None] + latter[0], earlier[1] + latter[1])

    incoming, _ = carried_in(
        (local_state, ending), "seq", combine, (zero_state, jnp.zeros_like(ending))
    )
    scores = (
        jnp.einsum("thd,shd->hts", query_heads, key_heads, preferred_element_type=jnp.float32)
        * scaling
    )
    spacing = running.T[:, :, None] - running.T[:, None, :]
    causal = jnp.arange(length)[:, None] >= jnp.arange(length)[None, :]
    decay_mask = jnp.where(causal[None], jnp.exp(jnp.minimum(spacing, 0.0)), 0.0)
    attend_weights = (scores * decay_mask).astype(jnp.bfloat16)
    within = jnp.einsum(
        "hts,shd->thd", attend_weights, value_heads, preferred_element_type=jnp.float32
    )
    query_scaled = (
        query_heads.astype(jnp.float32) * (jnp.exp(running) * scaling)[:, :, None]
    ).astype(jnp.bfloat16)
    across = jnp.einsum(
        "thd,hde->the",
        query_scaled,
        incoming.astype(jnp.bfloat16),
        preferred_element_type=jnp.float32,
    )
    unnormed = within + across
    spread = jnp.mean(unnormed * unnormed, axis=2, keepdims=True)
    normed = (
        (unnormed * lax.rsqrt(spread + 1e-06)).astype(jnp.bfloat16).reshape(length, model_width)
    )
    attended = jnp.dot(
        normed,
        lax.all_gather(out_weight, "seq", axis=0, tiled=True),
        preferred_element_type=jnp.float32,
    )
    residual = (stream.astype(jnp.float32) + attended).astype(jnp.bfloat16)
    widened = residual.astype(jnp.float32)
    mixed_in = (
        widened * lax.rsqrt(jnp.mean(widened * widened, axis=1, keepdims=True) + 1e-06) * moe_gain
    ).astype(jnp.bfloat16)
    offsets = token_index - device * length
    picked = jnp.take(mixed_in, offsets, axis=0)
    arrived = lax.all_to_all(picked, "seq", split_axis=0, concat_axis=0, tiled=True)
    gating = jnp.einsum("snd,df->snf", arrived, gate_weight[0], preferred_element_type=jnp.float32)
    upward = jnp.einsum("snd,df->snf", arrived, up_weight[0], preferred_element_type=jnp.float32)
    activated = (jax.nn.silu(gating) * upward).astype(jnp.bfloat16)
    produced = jnp.einsum(
        "snf,fd->snd", activated, down_weight[0], preferred_element_type=jnp.float32
    ).astype(jnp.bfloat16)
    returned = lax.all_to_all(produced, "seq", split_axis=0, concat_axis=0, tiled=True)
    scaled = returned.astype(jnp.float32) * route_weight[:, :, None]
    total = widened.at[offsets.reshape(-1)].add(scaled.reshape(-1, model_width))
    return total.astype(jnp.bfloat16)


def solution(mesh):
    placed = (
        P(("dp", "seq"), None),
        P(("dp", "seq"), None),
        P(("dp", "seq"), None),
        P(("dp", "seq"), None),
        P(("dp", "seq"), None),
        P("dp", "seq"),
        P("dp", "seq"),
        P(),
        P("seq", None),
        P("seq", None, None),
        P("seq", None, None),
        P("seq", None, None),
    )
    return jax.shard_map(
        shards, mesh=mesh, in_specs=placed, out_specs=P(("dp", "seq"), None), check_vma=False
    )
```

profile of v0, /device:TPU:1, one launch (start us, length us, event | category | flops | bytes accessed | tf_op | source)
XLA Modules:
  0.0 257.3 jit_solution(80279382773358347)
XLA Ops:
  8.8 1.9 copy.50
  10.7 3.4 %fusion.31 = bf16[16,128,128]{2,1,0:T(8,128)(2,1)} fusion(bf16[384,16,128]{0,2,1:T(8,128)(2,1)S(1)} %bitcast.105, f32[384,16]{0,1:T(8,128)S(1)} %get-tuple-element.132, bf16[384,2048]{1,0:T(8,128)(2,1)} %param.16), kind=kOutput, calls=%fused_computation.40 | convolution fusion | flops 203948032 | bytes 3694592 | tf_op jit(solution)/shard_map/shd,she->hde/dot_general | solution.py:56
  15.1 10.1 %all-gather.1 = bf16[8,1,16]{2,1,0:T(2,128)(2,1)S(1)} all-gather(bf16[1,1,16]{2,1,0:T(2,128)(2,1)S(1)} %bitcast.110), channel_id=1, replica_groups=mesh['dp'=4,'seq'=8] {'seq'}, dimensions={0}, use_global_device_ids=true | all-gather | bytes 288 | tf_op jit(solution)/shard_map/all_gather | solution.py:10
  25.4 28.2 %all-gather.7.cloned.1.call-done = bf16[128,128,128]{2,1,0:T(8,128)(2,1)} async-done(((bf16[16,128,128]{2,1,0:T(8,128)(2,1)}), bf16[128,128,128]{2,1,0:T(8,128)(2,1)}) %all-gather.7.cloned.1.call-update) | async-done | bytes 4194320 | tf_op jit(solution)/shard_map/all_gather | solution.py:10
  53.6 10.7 %while.14 = (s32[]{:T(128)}, f32[16,128,128]{2,1,0:T(8,128)S(1)}, s32[]{:T(128)}, bf16[8,16]{1,0:T(8,128)(2,1)S(1)}, bf16[8,16,128,128]{3,2,1,0:T(8,128)(2,1)}, /*index=5*/s32[]{:T(128)}, s32[]{:T(128)}) while((s32[]{:T(128)}, f32[16,128,128]{2,1,0:T(8,128)S(1)}, s32[]{:T(128)}, bf16[8,16]{1,0:T(8,128)(2,1)S(1)}, ...), condition=%wide.region_3.4_spmd.clone, body=%wide.region_2.3_spmd.clone.sunk | while | flops 1310740 | bytes 2621705 | solution.py:27
  61.6 1.3 fusion.54
  62.9 1.4 fusion.54
  64.3 2.8 %fusion.18 = f32[16,128,384]{2,1,0:T(8,128)} fusion(f32[384,16]{0,1:T(8,128)S(1)} %get-tuple-element.133, f32[16,128,128]{2,1,0:T(8,128)S(1)} %get-tuple-element.99, bf16[384,2048]{1,0:T(8,128)(2,1)S(1)} %copy-done), kind=kOutput, calls=%fused_computation.29 | convolution fusion | flops 203948032 | bytes 5791744 | tf_op jit(solution)/shard_map/thd,hde->the/dot_general | solution.py:81
  67.1 7.5 %multiply_reduce_fusion.1 = (f32[384,16]{0,1:T(8,128)S(1)}, f32[384,16,128]{0,2,1:T(8,128)}) fusion(f32[16,128,384]{2,1,0:T(8,128)} %fusion.18, f32[16,384]{1,0:T(8,128)S(1)} %get-tuple-element.130, pred[384,384]{1,0:T(8,128)(4,1)S(1)} %iota_compare_fusion, bf16[384,16,128]{0,2,1:T(8,128)(2,1)} %bitcast.106, bf16[384,2048]{1,0:T(8,128)(2,1)} %param.16, ...), kind=kOutput, calls=%fused_computation.23 | convolution fusion | flops 1224468480 | bytes 11206656 | tf_op jit(solution)/shard_map/hts,shd->thd/dot_general | solution.py:75
  74.7 2.3 multiply_convert_fusion.4
  77.0 32.8 %all-gather.5.cloned.1.call-done = bf16[2048,2048]{1,0:T(8,128)(2,1)} async-done(((bf16[256,2048]{1,0:T(8,128)(2,1)}), bf16[2048,2048]{1,0:T(8,128)(2,1)}) %all-gather.5.cloned.1.call-update) | async-done | bytes 8388624 | tf_op jit(solution)/shard_map/all_gather | solution.py:94
  109.9 6.0 %multiply_reduce_fusion = (f32[384]{0:T(512)S(1)}, f32[384,2048]{1,0:T(8,128)S(1)}) fusion(bf16[384,2048]{0,1:T(8,128)(2,1)S(1)} %bitcast.103, bf16[2048,2048]{1,0:T(8,128)(2,1)} %all-gather.5.cloned.1.call-done, bf16[384,2048]{1,0:T(8,128)(2,1)S(1)} %copy-done.3), kind=kOutput, calls=%fused_computation.20 | convolution fusion | flops 3225943552 | bytes 14681600 | tf_op jit(solution)/shard_map/dot_general | solution.py:92
  115.9 1.7 copy-done.2
  117.9 4.3 %gather_fusion = bf16[768,2048]{1,0:T(8,128)(2,1)} fusion(bf16[384,2048]{1,0:T(8,128)(2,1)S(1)} %multiply_convert_fusion.3, s32[1024]{0:T(1024)S(1)} %pad_clamp_fusion), kind=kCustom, calls=%fused_computation | custom fusion | bytes 6294528 | tf_op jit(solution)/shard_map/jit(_take)/gather | solution.py:103
  122.2 2.2 broadcast_select_fusion
  124.4 39.6 %all_to_all.10 = bf16[8,96,2048]{2,1,0:T(8,128)(2,1)S(1)} all-to-all(bf16[8,96,2048]{2,1,0:T(8,128)(2,1)S(1)} %broadcast_select_fusion), channel_id=1, replica_groups=mesh['dp'=4,'seq'=8] {'seq'}, dimensions={0} | all-to-all | bytes 6291456 | tf_op jit(solution)/shard_map/all_to_all | solution.py:104
  164.0 7.7 %fusion.3 = f32[8,96,1408]{2,1,0:T(8,128)S(1)} fusion(bf16[8,96,2048]{2,1,0:T(8,128)(2,1)S(1)} %all_to_all.10, bf16[1,2048,1408]{2,1,0:T(8,128)(2,1)} %param.24), kind=kOutput, calls=%fused_computation.9 | convolution fusion | flops 4429185024 | bytes 13238272 | tf_op jit(solution)/shard_map/snd,df->snf/dot_general | solution.py:106
  171.7 5.7 %multiply_convert_fusion.2 = bf16[8,96,1408]{2,1,0:T(8,128)(2,1)S(1)} fusion(f32[8,96,1408]{2,1,0:T(8,128)S(1)} %fusion.3, bf16[8,96,2048]{2,1,0:T(8,128)(2,1)S(1)} %all_to_all.10, bf16[1,2048,1408]{2,1,0:T(8,128)(2,1)S(1)} %bitcast.112), kind=kOutput, calls=%fused_computation.15 | convolution fusion | flops 4435673088 | bytes 15400960 | tf_op jit(solution)/shard_map/snd,df->snf/dot_general | solution.py:105
  177.4 6.4 %fusion.11 = bf16[8,96,2048]{2,1,0:T(8,128)(2,1)} fusion(bf16[8,96,1408]{2,1,0:T(8,128)(2,1)S(1)} %multiply_convert_fusion.2, bf16[1,1408,2048]{2,1,0:T(8,128)(2,1)S(1)} %bitcast.114), kind=kOutput, calls=%fused_computation.16 | convolution fusion | flops 4430757888 | bytes 11075584 | tf_op jit(solution)/shard_map/snf,fd->snd/dot_general | solution.py:108
  183.9 5.8 %all-to-all-start.1 = ((bf16[8,96,2048]{2,1,0:T(8,128)(2,1)}), bf16[8,96,2048]{2,1,0:T(8,128)(2,1)}, u32[]{:S(2)}, u32[]{:S(2)}) async-start(bf16[8,96,2048]{2,1,0:T(8,128)(2,1)} %fusion.11), calls=%async_computation.1 | async-start | bytes 6291456 | tf_op jit(solution)/shard_map/all_to_all | solution.py:111
  189.8 34.1 %all-to-all-done.1 = bf16[8,96,2048]{2,1,0:T(8,128)(2,1)} async-done(((bf16[8,96,2048]{2,1,0:T(8,128)(2,1)}), bf16[8,96,2048]{2,1,0:T(8,128)(2,1)}, u32[]{:S(2)}, u32[]{:S(2)}) %all-to-all-start.1) | async-done | bytes 3145760 | tf_op jit(solution)/shard_map/all_to_all | solution.py:111
  223.9 5.0 %convert_multiply_fusion = f32[8,96,2048]{2,1,0:T(8,128)} fusion(bf16[8,96,2048]{2,1,0:T(8,128)(2,1)} %all-to-all-done.1, f32[8,96]{1,0:T(8,128)S(1)} %copy-done.6), kind=kLoop, calls=%fused_computation.6 | loop fusion | flops 3145728 | bytes 9440256 | tf_op jit(solution)/shard_map/mul | solution.py:112
  228.9 18.3 %scatter_fusion = f32[384,2048]{1,0:T(8,128)} fusion(f32[384,2048]{1,0:T(8,128)} %copy-done.2, s32[768]{0:T(1024)S(1)} %fusion.36, f32[768,2048]{1,0:T(8,128)} %bitcast.101), kind=kCustom, calls=%fused_computation.1 | custom fusion | flops 1572864 | bytes 18877440 | tf_op jit(solution)/shard_map/scatter-add | solution.py:113
  247.2 3.3 %convert_element_type.90 = bf16[384,2048]{1,0:T(8,128)(2,1)} convert(f32[384,2048]{1,0:T(8,128)} %scatter_fusion) | non-fusion elementwise | flops 786432 | bytes 4718592 | tf_op jit(solution)/shard_map/convert_element_type | solution.py:114
  (63 shorter events, 11.7 us)
Async XLA Ops:
  6.5 57.8 %copy-start = (bf16[384,2048]{1,0:T(8,128)(2,1)S(1)}, bf16[384,2048]{1,0:T(8,128)(2,1)}, u32[]{:S(2)}) copy-start(bf16[384,2048]{1,0:T(8,128)(2,1)} %param.14) | copy-start | bytes 4718596
  6.5 47.0 %all-gather.7.cloned.1.call-start = ((), (), s32[]{:S(2)}) async-start(), calls=%async_computation.3 | async-start | bytes 4718592 | tf_op jit(solution)/shard_map/all_gather | solution.py:10
  10.7 4.2 %copy-start.4 = (bf16[384,2048]{0,1:T(8,128)(2,1)}, bf16[384,2048]{0,1:T(8,128)(2,1)S(1)}, u32[]{:S(2)}) copy-start(bf16[384,2048]{0,1:T(8,128)(2,1)S(1)} %copy.50) | copy-start | bytes 4718596
  10.7 14.5 %copy-start.7 = (s32[8,96]{1,0:T(8,128)S(1)}, s32[8,96]{1,0:T(8,128)}, u32[]{:S(2)}) copy-start(s32[8,96]{1,0:T(8,128)} %param.19) | copy-start | bytes 9220
  14.2 95.7 %all-gather.5.cloned.1.call-start = ((), (), s32[]{:S(2)}) async-start(), calls=%async_computation.2 | async-start | bytes 9437184 | tf_op jit(solution)/shard_map/all_gather | solution.py:94
  74.7 35.2 %copy-start.3 = (bf16[384,2048]{1,0:T(8,128)(2,1)S(1)}, bf16[384,2048]{1,0:T(8,128)(2,1)}, u32[]{:S(2)}) copy-start(bf16[384,2048]{1,0:T(8,128)(2,1)} %param.17) | copy-start | bytes 4718596
  109.9 7.7 %copy-start.5 = (f32[2048]{0:T(1024)S(1)}, f32[2048]{0:T(1024)}, u32[]{:S(2)}) copy-start(f32[2048]{0:T(1024)} %param.21) | copy-start | bytes 24580
  115.9 1.7 copy-start.2
  124.4 47.2 %slice-start = ((s8[5767168]{0:T(1024)(128)(4,1)}), s8[4194304]{0:T(1024)(128)(4,1)S(1)}, s32[]{:S(2)}) async-start(s8[5767168]{0:T(1024)(128)(4,1)} %bitcast.111), calls=%async_computation.4 | async-start | bytes 8388608
  164.0 7.7 %slice-start.1 = ((s8[5767168]{0:T(1024)(128)(4,1)}), s8[1572864]{0:T(1024)(128)(4,1)S(1)}, s32[]{:S(2)}) async-start(s8[5767168]{0:T(1024)(128)(4,1)} %bitcast.111), calls=%async_computation.5 | async-start | bytes 3145728
  164.0 13.4 %slice-start.2 = ((s8[5767168]{0:T(1024)(128)(4,1)}), s8[4194304]{0:T(1024)(128)(4,1)S(1)}, s32[]{:S(2)}) async-start(s8[5767168]{0:T(1024)(128)(4,1)} %bitcast.113), calls=%async_computation.6 | async-start | bytes 8388608
  171.7 5.7 %slice-start.3 = ((s8[5767168]{0:T(1024)(128)(4,1)}), s8[1572864]{0:T(1024)(128)(4,1)S(1)}, s32[]{:S(2)}) async-start(s8[5767168]{0:T(1024)(128)(4,1)} %bitcast.113), calls=%async_computation.7 | async-start | bytes 3145728
  183.9 40.0 %copy-start.6 = (f32[8,96]{1,0:T(8,128)S(1)}, f32[8,96]{1,0:T(8,128)}, u32[]{:S(2)}) copy-start(f32[8,96]{1,0:T(8,128)} %param.20) | copy-start | bytes 9220
  183.9 40.0 %all-to-all-start.1 = ((bf16[8,96,2048]{2,1,0:T(8,128)(2,1)}), bf16[8,96,2048]{2,1,0:T(8,128)(2,1)}, u32[]{:S(2)}, u32[]{:S(2)}) async-start(bf16[8,96,2048]{2,1,0:T(8,128)(2,1)} %fusion.11), calls=%async_computation.1 | async-start | bytes 6291456 | tf_op jit(solution)/shard_map/all_to_all | solution.py:111
  228.9 21.6 %copy-start.1 = (bf16[384,2048]{1,0:T(8,128)(2,1)S(1)}, bf16[384,2048]{1,0:T(8,128)(2,1)}, u32[]{:S(2)}) copy-start(bf16[384,2048]{1,0:T(8,128)(2,1)} %param.14) | copy-start | bytes 4718596
Sparse Core Ops, SparseCore 0:
  14.3 39.2 all-gather.6
  55.4 54.3 all-gather.4
where the time goes:
time: 262 us; the launch traced here: 257 us
  waiting for transfers between devices  95.9 us (37%)
  blocking collectives  49.6 us (19%)
  other arithmetic  43.2 us (16%)
  matrix products  39.6 us (15%)
  between operations  13.6 us (5%)
  local copies, waits for them, and re-layouts  9.4 us (4%)
  starting transfers between devices  5.83 us (2%)
    all_to_all x1, blocking collectives, shards(): lax.all_to_all(picked, 'seq', split_axis=0, concat_axis=0, tiled=True)  39.6 us
    all_to_all x1, waiting for transfers between devices, shards(): lax.all_to_all(produced, 'seq', split_axis=0, concat_axis=0, tiled=True)  34.1 us
    all_gather x1, waiting for transfers between devices, shards(): lax.all_gather(out_weight, 'seq', axis=0, tiled=True)  32.8 us
    all_gather x1, waiting for transfers between devices, carried_in(): lax.all_gather(part.astype(kind), axis)  28.2 us
    scatter-add x1, other arithmetic, shards(): total = widened.at[offsets.reshape(-1)].add(scaled.reshape(-1, model_width))  18.3 us
    select_n x8, other arithmetic, turn(): return jax.tree.map(lambda a, b: jnp.where(reached, a, b), new, before)  10.4 us
    all_gather x1, blocking collectives, carried_in(): lax.all_gather(part.astype(kind), axis)  10.1 us
    dot_general x1, matrix products, shards(): jnp.einsum('snd,df->snf', arrived, up_weight[0], preferred_element_type=j...  7.66 us
  transfers between devices with their start and end apart: 3, of which 3 were waited for; matrix products, arithmetic and copies ran while one was open for 9% of the time, Pallas kernels for 0%

commit v1 on v0

v1 whole, which is shorter than its diff:
```python
import functools

import jax
import jax.numpy as jnp
from jax import lax
from jax.experimental import pallas as pl
from jax.experimental.pallas import tpu as pltpu
from jax.sharding import PartitionSpec as P

MESH = pl.DeviceIdType.MESH
F32, BF16 = jnp.float32, jnp.bfloat16
EXACT = lax.Precision.HIGHEST


def flipped(index, offset):
    bit = 1
    while bit <= offset:
        if offset & bit:
            index = index + bit * (1 - 2 * ((index // bit) % 2))
        bit *= 2
    return index


def remote(src, dst, send, recv, peer):
    return pltpu.make_async_remote_copy(
        src_ref=src, dst_ref=dst, send_sem=send, recv_sem=recv,
        device_id={"seq": peer}, device_id_type=MESH,
    )


def greet(n, me):
    barrier = pltpu.get_barrier_semaphore()
    for offset in range(1, n):
        pl.semaphore_signal(
            barrier, inc=1, device_id={"seq": flipped(me, offset)}, device_id_type=MESH
        )
    pl.semaphore_wait(barrier, n - 1)


def attend_kernel(
    n, heads, size,
    q_h, k_h, v_h, s_h, ld, ldt, gain, w_h,
    res, mix,
    q, k, v, stream, weight, att, normed, run, runt,
    state, state_low, state_mate, total, before, give, take, before_low, before_mate,
    incoming, ends, coef,
    load_sem, w_send, w_recv, e_send, e_recv, s_send, s_recv,
):
    me = lax.axis_index("seq")
    core, chip = me % 2, me // 2
    mate = flipped(me, 1)
    length, width = q.shape
    rows = w_h.shape[0]
    half = heads // 2
    low = rows // 2
    bits = n.bit_length() - 2
    scaling = size ** (-0.5)

    loads = [
        pltpu.make_async_copy(src, dst, load_sem.at[i])
        for i, (src, dst) in enumerate(((k_h, k), (v_h, v), (q_h, q), (s_h, stream)))
    ]
    own_rows = pl.ds(pl.multiple_of(me * rows, rows), rows)
    loads.append(pltpu.make_async_copy(w_h, weight.at[own_rows], load_sem.at[4]))
    for copy in loads:
        copy.start()
    greet(n, me)

    def part(offset, piece):
        start = flipped(me, offset) * rows
        if piece == 0:
            return pl.ds(pl.multiple_of(start, low), low)
        if piece == 1:
            return pl.ds(pl.multiple_of(start + low, low), low)
        return pl.ds(pl.multiple_of(start, rows), rows)

    def own(piece):
        return w_h.at[pl.ds(piece * low, low)] if piece < 2 else w_h

    def spread(slot, src, where, offset):
        return remote(src, weight.at[where], w_send.at[slot], w_recv.at[slot], flipped(me, offset))

    square = n == 8
    if square:
        first = [
            spread(0, own(0), part(0, 0), 2),
            spread(1, own(1), part(0, 1), 4),
        ]
        second = [
            spread(2, own(1), part(0, 1), 2),
            spread(3, own(0), part(0, 0), 4),
        ]
        onward = [
            spread(4, weight.at[part(2, 0)], part(2, 0), 4),
            spread(5, weight.at[part(4, 1)], part(4, 1), 2),
        ]
        across_own = [spread(6, own(2), part(0, 2), 1)]
        across = [
            spread(7 + i, weight.at[part(o, p)], part(o, p), 1)
            for i, (o, p) in enumerate(((2, 0), (4, 1), (2, 1), (4, 0), (6, 0), (6, 1)))
        ]
    else:
        others = range(2, n, 2)
        first = [spread(o, own(2), part(0, 2), o) for o in others]
        second, onward = [], []
        across_own = [spread(1, own(2), part(0, 2), 1)]
        across = [spread(o + 1, weight.at[part(o, 2)], part(o, 2), 1) for o in others]
    for copy in first + across_own:
        copy.start()

    wide = lax.broadcasted_iota(jnp.int32, (length, length), 0)
    tall = lax.broadcasted_iota(jnp.int32, (length, length), 1)
    lower = (wide >= tall).astype(F32)
    upper = (wide <= tall).astype(F32)
    run[...] = jnp.dot(lower, ld[...], precision=EXACT, preferred_element_type=F32)
    runt[...] = jnp.dot(ldt[...], upper, precision=EXACT, preferred_element_type=F32)
    ends[me] = jnp.dot(
        ldt[...], jnp.ones((length, size), F32), precision=EXACT, preferred_element_type=F32
    )
    tell = [
        remote(ends.at[me], ends.at[me], e_send.at[o], e_recv.at[o], flipped(me, o))
        for o in range(1, n)
    ]
    for copy in tell:
        copy.start()

    def column(h, lanes):
        pick = (lax.broadcasted_iota(jnp.int32, (heads, lanes), 0) == h).astype(F32)
        return jnp.dot(run[...], pick, precision=EXACT, preferred_element_type=F32)

    def lanes_of(h):
        return pl.ds(pl.multiple_of(h * size, size), size)

    loads[0].wait()
    loads[1].wait()

    @pl.loop(0, heads)
    def _(h):
        shrink = jnp.exp(ends[me, pl.ds(h, 1), :] - column(h, size))
        scaled = (k[:, lanes_of(h)].astype(F32) * shrink).astype(BF16)
        new = lax.dot_general(
            scaled, v[:, lanes_of(h)], (((0,), (0,)), ((), ())), preferred_element_type=F32
        )
        state[h] = new
        state_low[h] = new.astype(BF16)

    swap = remote(state_low, state_mate, s_send.at[0], s_recv.at[0], mate)
    swap.start()
    for copy in tell:
        copy.wait()
    swap.wait()

    first_end, last_end = ends[2 * chip], ends[2 * chip + 1]
    coef[0] = jnp.exp(last_end)

    @pl.loop(0, half)
    def _(j):
        h = core * half + j
        mine, theirs = state[h], state_mate[h].astype(F32)
        early = jnp.where(core == 0, mine, theirs)
        late = jnp.where(core == 0, theirs, mine)
        both = early * coef[0, pl.ds(h, 1), :] + late
        total[j] = both
        give[0, j] = both.astype(BF16)
        before[j] = jnp.zeros_like(both)

    def exchange(b):
        return remote(
            give.at[b], take.at[b], s_send.at[b + 1], s_recv.at[b + 1], flipped(me, 2 << b)
        )

    def bit_of(b):
        return (me // (2 << b)) % 2

    def send_state(b):
        if b < bits - 1:
            exchange(b).start()
        else:

            @pl.when(bit_of(b) == 0)
            def _():
                exchange(b).start()

    send_state(0)
    for copy in second:
        copy.start()
    loads[2].wait()

    def attend(h):
        weights = lax.dot_general(
            q[:, lanes_of(h)], k[:, lanes_of(h)], (((1,), (1,)), ((), ())),
            preferred_element_type=F32,
        ) * scaling
        spacing = column(h, length) - runt[pl.ds(h, 1), :]
        decay = jnp.where(wide >= tall, jnp.exp(jnp.minimum(spacing, 0.0)), 0.0)
        att[:, lanes_of(h)] = jnp.dot(
            (weights * decay).astype(BF16), v[:, lanes_of(h)], preferred_element_type=F32
        )

    pl.loop(0, heads)(attend)

    group, ahead = first_end + last_end, jnp.zeros_like(first_end)
    for b in range(bits):
        base = (flipped(me, 2 << b) // (2 << b)) * (2 << b)
        other = ends[base]
        for i in range(1, 2 << b):
            other = other + ends[base + i]
        bit = bit_of(b)
        coef[0] = jnp.exp(ahead)
        coef[1] = jnp.where(bit == 1, jnp.exp(group), 1.0)
        coef[2] = jnp.where(bit == 1, 1.0, jnp.exp(other))
        if b < bits - 1:
            exchange(b).wait()
        else:

            @pl.when(bit == 0)
            def _():
                exchange(b).wait_send()

            @pl.when(bit == 1)
            def _():
                exchange(b).wait_recv()

        @pl.when(bit == 1)
        def _():
            @pl.loop(0, half)
            def _(j):
                h = core * half + j
                before[j] += take[b, j].astype(F32) * coef[0, pl.ds(h, 1), :]

        if b < bits - 1:

            @pl.loop(0, half)
            def _(j):
                h = core * half + j
                both = (
                    take[b, j].astype(F32) * coef[1, pl.ds(h, 1), :]
                    + total[j] * coef[2, pl.ds(h, 1), :]
                )
                total[j] = both
                give[b + 1, j] = both.astype(BF16)

            send_state(b + 1)
        ahead = ahead + jnp.where(bit == 1, other, 0.0)
        group = group + other
        if b == 0 and square:
            first[0].wait_recv()
            onward[0].start()
            across[0].start()
            first[1].wait_recv()
            onward[1].start()
            across[1].start()

    before_low[...] = before[...].astype(BF16)
    trade = remote(before_low, before_mate, s_send.at[bits + 1], s_recv.at[bits + 1], mate)
    trade.start()
    trade.wait()
    coef[0] = jnp.where(core == 1, jnp.exp(first_end), 1.0)

    @pl.loop(0, half)
    def _(j):
        for h, earlier in (
            (core * half + j, before[j]),
            ((1 - core) * half + j, before_mate[j].astype(F32)),
        ):
            mate_part = jnp.where(core == 1, state_mate[h].astype(F32), 0.0)
            incoming[h] = (earlier * coef[0, pl.ds(h, 1), :] + mate_part).astype(BF16)

    @pl.loop(0, heads)
    def _(h):
        grown = jnp.exp(column(h, size)) * scaling
        scaled = (q[:, lanes_of(h)].astype(F32) * grown).astype(BF16)
        whole = att[:, lanes_of(h)] + jnp.dot(scaled, incoming[h], preferred_element_type=F32)
        mean = jnp.mean(whole * whole, axis=1, keepdims=True)
        normed[:, lanes_of(h)] = (whole * lax.rsqrt(mean + 1e-06)).astype(BF16)

    tile = 512

    def project(offset, fresh):
        start = (flipped(me, offset) // 2) * (2 * rows)
        inner = pl.ds(pl.multiple_of(start, 2 * rows), 2 * rows)

        @pl.loop(0, width // tile)
        def _(i):
            cols = pl.ds(pl.multiple_of(i * tile, tile), tile)
            term = jnp.dot(normed[:, inner], weight[inner, cols], preferred_element_type=F32)
            att[:, cols] = term if fresh else att[:, cols] + term

    loads[4].wait()
    across_own[0].wait()
    project(0, True)
    if square:
        second[0].wait_recv()
        across[2].start()
        second[1].wait_recv()
        across[3].start()
        across[0].wait()
        across[2].wait()
        project(2, False)
        across[1].wait()
        across[3].wait()
        project(4, False)
        onward[0].wait_recv()
        across[4].start()
        onward[1].wait_recv()
        across[5].start()
        loads[3].wait()
        across[4].wait()
        across[5].wait()
        project(6, False)
        for copy in first + second + onward:
            copy.wait_send()
    else:
        for i, copy in enumerate(first):
            copy.wait()
            across[i].start()
        loads[3].wait()
        for i, offset in enumerate(range(2, n, 2)):
            across[i].wait()
            project(offset, False)

    step = 64

    @pl.loop(0, length // step)
    def _(i):
        at = pl.ds(pl.multiple_of(i * step, step), step)
        kept = (stream[at, :].astype(F32) + att[at, :]).astype(BF16)
        res[at, :] = kept
        kept = kept.astype(F32)
        mean = jnp.mean(kept * kept, axis=1, keepdims=True)
        mix[at, :] = (kept * lax.rsqrt(mean + 1e-06) * gain[...]).astype(BF16)


def expert_kernel(
    n, slots,
    mix, res, tok_col, tok_row, route, gate_h, up_h, down_h,
    out,
    gate, up, down, picked, arrived, hidden, produced, returned,
    load_sem, a_send, a_recv, b_send, b_recv,
):
    me = lax.axis_index("seq")
    length, width = mix.shape
    inner = gate.shape[1]
    loads = [
        pltpu.make_async_copy(src, dst, load_sem.at[i])
        for i, (src, dst) in enumerate(((gate_h, gate), (up_h, up), (down_h, down)))
    ]
    for copy in loads:
        copy.start()
    greet(n, me)

    def block(first, count=1):
        return pl.ds(first * slots, count * slots)

    def pick(first, count, into):
        lines = block(first, count)
        places = lax.broadcasted_iota(jnp.int32, (count * slots, length), 1)
        chosen = (tok_col[lines, :] == places).astype(F32).astype(BF16)
        tile = 512

        @pl.loop(0, width // tile)
        def _(i):
            cols = pl.ds(pl.multiple_of(i * tile, tile), tile)
            into[lines, cols] = jnp.dot(
                chosen, mix[:, cols], preferred_element_type=F32
            ).astype(BF16)

    def out_copy(o):
        return remote(
            picked.at[block(o)], arrived.at[block(o)], a_send.at[o], a_recv.at[o], flipped(me, o)
        )

    def back_copy(o):
        return remote(
            produced.at[block(o)], returned.at[block(o)], b_send.at[o], b_recv.at[o],
            flipped(me, o),
        )

    def expert(first, count):
        lines = block(first, count)
        tile = 256

        def upward(cols):
            x = arrived[lines, :]
            a = jnp.dot(x, gate[:, cols], preferred_element_type=F32)
            b = jnp.dot(x, up[:, cols], preferred_element_type=F32)
            hidden[lines, cols] = (a / (1.0 + jnp.exp(-a)) * b).astype(BF16)

        @pl.loop(0, inner // tile)
        def _(i):
            upward(pl.ds(pl.multiple_of(i * tile, tile), tile))

        if inner % tile:
            upward(pl.ds(inner - inner % tile, inner % tile))

        wide = 512

        @pl.loop(0, width // wide)
        def _(i):
            cols = pl.ds(pl.multiple_of(i * wide, wide), wide)
            produced[lines, cols] = jnp.dot(
                hidden[lines, :], down[:, cols], preferred_element_type=F32
            ).astype(BF16)

    near = list(range(2, n - n // 4))
    far = list(range(n - n // 4, n))
    pick(2, len(near), picked)
    for o in near:
        out_copy(o).start()
    pick(1, 1, picked)
    out_copy(1).start()
    pick(0, 1, arrived)
    pick(far[0], len(far), picked)
    for copy in loads:
        copy.wait()
    out_copy(1).wait()
    expert(0, 2)
    back_copy(1).start()
    returned[block(0), :] = produced[block(0), :]
    for o in near:
        out_copy(o).wait_send()
    for o in far:
        out_copy(o).start()
    for o in near:
        out_copy(o).wait_recv()
    expert(2, len(near))
    for o in near:
        back_copy(o).start()
    for o in far:
        out_copy(o).wait()
    expert(far[0], len(far))
    for o in far:
        back_copy(o).start()

    for o in range(1, n):
        back_copy(o).wait()
    lines = lax.broadcasted_iota(jnp.int32, (length, n * slots), 0)
    mixing = jnp.where(tok_row[...] == lines, route[...], 0.0).astype(BF16)
    tile = 512

    @pl.loop(0, width // tile)
    def _(i):
        cols = pl.ds(pl.multiple_of(i * tile, tile), tile)
        gathered = jnp.dot(mixing, returned[:, cols], preferred_element_type=F32)
        out[:, cols] = (res[:, cols].astype(F32) + gathered).astype(BF16)


def by_offset(array, n, device):
    axes = n.bit_length() - 1
    cut = array.reshape((2,) * axes + array.shape[1:])
    for axis in range(axes):
        bit = (device // (n >> (axis + 1))) % 2
        cut = jnp.where(bit == 1, jnp.flip(cut, axis), cut)
    return cut.reshape(array.shape)


def shards(
    queries, keys_in, values, stream, log_decay, token_index, route_weight, moe_gain,
    out_weight, gate_weight, up_weight, down_weight,
):
    n = lax.axis_size("seq")
    device = lax.axis_index("seq")
    length, width = queries.shape
    heads = log_decay.shape[1]
    size = width // heads
    half = heads // 2
    bits = n.bit_length() - 2
    inner = gate_weight.shape[2]
    vmem = pl.BlockSpec(memory_space=pltpu.VMEM)
    anywhere = pl.BlockSpec(memory_space=pl.ANY)
    dma = pltpu.SemaphoreType.DMA
    rows_of = jax.ShapeDtypeStruct((length, width), BF16)

    residual, mixed_in = pl.pallas_call(
        functools.partial(attend_kernel, n, heads, size),
        out_shape=(rows_of, rows_of),
        in_specs=[anywhere] * 4 + [vmem] * 3 + [anywhere],
        out_specs=(vmem, vmem),
        scratch_shapes=[
            pltpu.VMEM((length, width), BF16),
            pltpu.VMEM((length, width), BF16),
            pltpu.VMEM((length, width), BF16),
            pltpu.VMEM((length, width), BF16),
            pltpu.VMEM((width, width), BF16),
            pltpu.VMEM((length, width), F32),
            pltpu.VMEM((length, width), BF16),
            pltpu.VMEM((length, heads), F32),
            pltpu.VMEM((heads, length), F32),
            pltpu.VMEM((heads, size, size), F32),
            pltpu.VMEM((heads, size, size), BF16),
            pltpu.VMEM((heads, size, size), BF16),
            pltpu.VMEM((half, size, size), F32),
            pltpu.VMEM((half, size, size), F32),
            pltpu.VMEM((bits, half, size, size), BF16),
            pltpu.VMEM((bits, half, size, size), BF16),
            pltpu.VMEM((half, size, size), BF16),
            pltpu.VMEM((half, size, size), BF16),
            pltpu.VMEM((heads, size, size), BF16),
            pltpu.VMEM((n, heads, size), F32),
            pltpu.VMEM((3, heads, size), F32),
            dma((5,)),
            dma((max(n, 13),)),
            dma((max(n, 13),)),
            dma((n,)),
            dma((n,)),
            dma((bits + 2,)),
            dma((bits + 2,)),
        ],
        compiler_params=pltpu.CompilerParams(
            collective_id=0, has_side_effects=True, vmem_limit_bytes=48 * 2**20
        ),
        cost_estimate=pl.CostEstimate(
            flops=2 * length * width * width, bytes_accessed=12 * length * width, transcendentals=0
        ),
        name="attend",
    )(
        queries, keys_in, values, stream, log_decay, log_decay.T, moe_gain[None, :], out_weight
    )

    chosen = token_index.shape[1]
    slots = -(-chosen // 16) * 16
    fill = ((0, 0), (0, slots - chosen))
    places = jnp.pad(token_index - device * length, fill, constant_values=-1)
    places = by_offset(places, n, device)
    route = by_offset(jnp.pad(route_weight, fill), n, device).reshape(1, n * slots)

    return pl.pallas_call(
        functools.partial(expert_kernel, n, slots),
        out_shape=rows_of,
        in_specs=[vmem] * 5 + [anywhere] * 3,
        out_specs=vmem,
        scratch_shapes=[
            pltpu.VMEM((width, inner), BF16),
            pltpu.VMEM((width, inner), BF16),
            pltpu.VMEM((inner, width), BF16),
            pltpu.VMEM((n * slots, width), BF16),
            pltpu.VMEM((n * slots, width), BF16),
            pltpu.VMEM((n * slots, inner), BF16),
            pltpu.VMEM((n * slots, width), BF16),
            pltpu.VMEM((n * slots, width), BF16),
            dma((3,)),
            dma((n,)),
            dma((n,)),
            dma((n,)),
            dma((n,)),
        ],
        compiler_params=pltpu.CompilerParams(
            collective_id=1, has_side_effects=True, vmem_limit_bytes=56 * 2**20
        ),
        cost_estimate=pl.CostEstimate(
            flops=6 * n * slots * width * inner, bytes_accessed=6 * width * inner, transcendentals=0
        ),
        name="experts",
    )(
        mixed_in, residual, places.reshape(n * slots, 1), places.reshape(1, n * slots), route,
        gate_weight[0], up_weight[0], down_weight[0],
    )


def solution(mesh):
    placed = (
        P(("dp", "seq"), None),
        P(("dp", "seq"), None),
        P(("dp", "seq"), None),
        P(("dp", "seq"), None),
        P(("dp", "seq"), None),
        P("dp", "seq"),
        P("dp", "seq"),
        P(),
        P("seq", None),
        P("seq", None, None),
        P("seq", None, None),
        P("seq", None, None),
    )
    return jax.shard_map(
        shards, mesh=mesh, in_specs=placed, out_specs=P(("dp", "seq"), None), check_vma=False
    )
```

time: 262 us -> 154 us (0.59); the launches traced: 257 us -> 154 us
  Pallas kernels: 0 us -> 140 us
  waiting for transfers between devices: 95.9 us -> 0 us
  blocking collectives: 49.6 us -> 0 us
  other arithmetic: 43.2 us -> 1.49 us
  matrix products: 39.6 us -> 0 us
  between operations: 13.6 us -> 0.04 us
  starting transfers between devices: 5.83 us -> 0 us
  local copies, waits for them, and re-layouts: 9.4 us -> 12.4 us
    pallas_call x0 -> x2, Pallas kernels: none -> 140 us  [the longest x1 79.1 us: shards(): pl.pallas_call(functools.partial(expert_kernel, n, slots), out_shape=rows...]
    all_gather x2 -> x0, waiting for transfers between devices: 61 us -> none  [the longest x1 32.8 us: shards(): lax.all_gather(out_weight, 'seq', axis=0, tiled=True)]
    all_to_all x1 -> x0, blocking collectives: 39.6 us -> none  [shards(): lax.all_to_all(picked, 'seq', split_axis=0, concat_axis=0, tiled=True)]
    dot_general x7 -> x0, matrix products: 39.6 us -> none  [the longest x1 7.66 us: shards(): jnp.einsum('snd,df->snf', arrived, up_weight[0], preferred_element_type=j...]
    all_to_all x1 -> x0, waiting for transfers between devices: 34.1 us -> none  [shards(): lax.all_to_all(produced, 'seq', split_axis=0, concat_axis=0, tiled=True)]
    scatter-add x1 -> x0, other arithmetic: 18.3 us -> none  [shards(): total = widened.at[offsets.reshape(-1)].add(scaled.reshape(-1, model_width))]
    select_n x11 -> x6, other arithmetic: 12.7 us -> 0.8 us  [by_offset(): cut = jnp.where(bit == 1, jnp.flip(cut, axis), cut)]
    all_gather x1 -> x0, blocking collectives: 10.1 us -> none  [carried_in(): lax.all_gather(part.astype(kind), axis)]
  transfers between devices with their start and end apart: 3 -> 0, of which waited for: 3 -> 0; matrix products, arithmetic and copies ran while one was open for 9% -> 0% of each run, Pallas kernels for 0% -> 0%
where the time goes in v1:
time: 154 us
  Pallas kernels  140 us (91%)
  local copies, waits for them, and re-layouts  12.4 us (8%)
    pallas_call x1, Pallas kernels, shards(): pl.pallas_call(functools.partial(expert_kernel, n, slots), out_shape=rows...  79.1 us
    pallas_call x1, Pallas kernels, shards(): pl.pallas_call(functools.partial(attend_kernel, n, heads, size), out_shap...  60.7 us
    unnamed x14, local copies, waits for them, and re-layouts  9.94 us

profile of v1, /device:TPU:1, one launch (start us, length us, event | category | flops | bytes accessed | tf_op | source)
XLA Modules:
  0.0 153.7 jit_solution(2730324203008475411)
XLA Ops:
  0.0 0.7 broadcast_subtract_fusion
  0.7 0.8 reverse_select_fusion.1
  1.5 0.7 reshape_reshape.11.route
  2.2 0.7 reshape_reshape.10.tok_row
  2.9 0.9 copy.14.ld
  3.8 1.0 reshape_reshape.12.tok_col
  4.8 0.0 copy-start
  4.8 0.7 copy-done
  5.5 0.0 copy-start.1
  5.5 1.4 copy-done.1
  6.9 0.0 copy-start.2
  6.9 1.2 copy-done.2
  8.2 0.0 copy-start.3
  8.2 0.7 copy-done.3
  8.9 60.7 %attend.1 = (bf16[384,2048]{1,0:T(8,128)(2,1)S(1)}, bf16[384,2048]{1,0:T(8,128)(2,1)S(1)}) custom-call(bf16[384,2048]{1,0:T(8,128)(2,1)S(1)} %copy-done.1, bf16[384,2048]{1,0:T(8,128)(2,1)} %k_h.1, bf16[384,2048]{1,0:T(8,128)(2,1)} %v_h.1, bf16[384,2048]{1,0:T(8,128)(2,1)} %s_h.1, f32[384,16]{1,0:T(8,128)S(1)} %copy.14.ld, f32[16,384]{1,0:T(8,128)S(1)} %bitcast.7, ...), custom_call_target="tpu_custom_call" | custom-call | flops 3221225472 | bytes 9437184 | tf_op jit(solution)/shard_map/attend/pallas_call | solution.py:474
  69.6 0.0 copy-start.4
  69.6 1.1 copy-done.4
  70.7 0.0 copy-start.5
  70.7 1.1 copy-done.5
  71.9 79.1 %experts.1 = bf16[384,2048]{1,0:T(8,128)(2,1)} custom-call(bf16[384,2048]{1,0:T(8,128)(2,1)} %copy-done.5, bf16[384,2048]{1,0:T(8,128)(2,1)} %copy-done.4, s32[768,1]{1,0:T(8,128)} %reshape_reshape.12.tok_col, s32[1,768]{1,0:T(1,128)} %reshape_reshape.10.tok_row, f32[1,768]{1,0:T(1,128)} %reshape_reshape.11.route, bf16[2048,1408]{1,0:T(8,128)(2,1)} %bitcast.11, ...), custom_call_target="tpu_custom_call" | custom-call | flops 13287555072 | bytes 17301504 | tf_op jit(solution)/shard_map/experts/pallas_call | solution.py:527
  150.9 2.7 %copy.17 = bf16[384,2048]{1,0:T(8,128)(2,1)} copy(bf16[384,2048]{1,0:T(8,128)(2,1)} %experts.1) | data formatting | bytes 3145728
  (7 shorter events, 0.1 us)
Async XLA Ops:
  4.8 0.7 copy-start
  5.5 1.4 copy-start.1
  6.9 1.2 copy-start.2
  8.2 0.7 copy-start.3
  69.6 1.2 copy-start.4
  70.7 1.1 copy-start.5

commit v2 on v1

--- a/solution.py
+++ b/solution.py
@@ -37,14 +37,17 @@
     pl.semaphore_wait(barrier, n - 1)
 
 
-def attend_kernel(
-    n, heads, size,
-    q_h, k_h, v_h, s_h, ld, ldt, gain, w_h,
-    res, mix,
-    q, k, v, stream, weight, att, normed, run, runt,
+def layer_kernel(
+    n, heads, size, slots,
+    q_h, k_h, v_h, s_h, ldt_h, gain_h, w_h, tok_h, route_h, gate_h, up_h, down_h,
+    out,
+    q, k, v, stream, ldt, gain, tok, route, gate, up, down,
+    weight, att, normed, run, runt,
     state, state_low, state_mate, total, before, give, take, before_low, before_mate,
     incoming, ends, coef,
+    arrived, hidden, returned,
     load_sem, w_send, w_recv, e_send, e_recv, s_send, s_recv,
+    a_send, a_recv, b_send, b_recv, o_sem,
 ):
     me = lax.axis_index("seq")
     core, chip = me % 2, me // 2
@@ -56,14 +59,17 @@
     bits = n.bit_length() - 2
     scaling = size ** (-0.5)
 
+    own_rows = pl.ds(pl.multiple_of(me * rows, rows), rows)
     loads = [
         pltpu.make_async_copy(src, dst, load_sem.at[i])
-        for i, (src, dst) in enumerate(((k_h, k), (v_h, v), (q_h, q), (s_h, stream)))
+        for i, (src, dst) in enumerate((
+            (k_h, k), (v_h, v), (q_h, q), (s_h, stream), (w_h, weight.at[own_rows]),
+            (ldt_h, ldt), (gain_h, gain), (tok_h, tok), (route_h, route),
+            (gate_h, gate), (up_h, up), (down_h, down),
+        ))
     ]
-    own_rows = pl.ds(pl.multiple_of(me * rows, rows), rows)
-    loads.append(pltpu.make_async_copy(w_h, weight.at[own_rows], load_sem.at[4]))
-    for copy in loads:
-        copy.start()
+    for i in (5, 0, 1, 2, 4, 3, 6, 7, 8):
+        loads[i].start()
     greet(n, me)
 
     def part(offset, piece):
@@ -112,7 +118,10 @@
     tall = lax.broadcasted_iota(jnp.int32, (length, length), 1)
     lower = (wide >= tall).astype(F32)
     upper = (wide <= tall).astype(F32)
-    run[...] = jnp.dot(lower, ld[...], precision=EXACT, preferred_element_type=F32)
+    loads[5].wait()
+    run[...] = lax.dot_general(
+        lower, ldt[...], (((1,), (1,)), ((), ())), precision=EXACT, preferred_element_type=F32
+    )
     runt[...] = jnp.dot(ldt[...], upper, precision=EXACT, preferred_element_type=F32)
     ends[me] = jnp.dot(
         ldt[...], jnp.ones((length, size), F32), precision=EXACT, preferred_element_type=F32
@@ -124,19 +133,37 @@
     for copy in tell:
         copy.start()
 
-    def column(h, lanes):
-        pick = (lax.broadcasted_iota(jnp.int32, (heads, lanes), 0) == h).astype(F32)
-        return jnp.dot(run[...], pick, precision=EXACT, preferred_element_type=F32)
+    def column(h):
+        here = lax.broadcasted_iota(jnp.int32, (length, heads), 1) == h
+        return jnp.sum(jnp.where(here, run[...], 0.0), axis=1, keepdims=True)
 
     def lanes_of(h):
         return pl.ds(pl.multiple_of(h * size, size), size)
 
+    chosen = tok.shape[1]
+
+    def flat(source, first, count, otherwise):
+        lanes = count * slots
+        slot = lax.broadcasted_iota(jnp.int32, (chosen, lanes), 0)
+        lane = lax.broadcasted_iota(jnp.int32, (chosen, lanes), 1)
+        line = lax.broadcasted_iota(jnp.int32, (n, lanes), 0)
+        along = lax.broadcasted_iota(jnp.int32, (n, lanes), 1)
+        spot = jnp.zeros((chosen, lanes), F32)
+        own_line = jnp.zeros((n, lanes), F32)
+        for i in range(count):
+            spot = jnp.where(lane == slot + i * slots, 1.0, spot)
+            within = (along >= i * slots) & (along < i * slots + chosen)
+            own_line = jnp.where(within & (line == flipped(me, first + i)), 1.0, own_line)
+        placed = jnp.dot(source, spot, precision=EXACT, preferred_element_type=F32) * own_line
+        filled = jnp.sum(own_line, axis=0, keepdims=True)
+        return jnp.sum(placed, axis=0, keepdims=True) + otherwise * (1.0 - filled)
+
     loads[0].wait()
     loads[1].wait()
 
     @pl.loop(0, heads)
     def _(h):
-        shrink = jnp.exp(ends[me, pl.ds(h, 1), :] - column(h, size))
+        shrink = jnp.exp(ends[me, pl.ds(h, 1), :] - column(h))
         scaled = (k[:, lanes_of(h)].astype(F32) * shrink).astype(BF16)
         new = lax.dot_general(
             scaled, v[:, lanes_of(h)], (((0,), (0,)), ((), ())), preferred_element_type=F32
@@ -182,19 +209,30 @@
                 exchange(b).start()
 
     send_state(0)
-    for copy in second:
+    for copy in second + loads[9:]:
         copy.start()
     loads[2].wait()
 
     def attend(h):
-        weights = lax.dot_general(
-            q[:, lanes_of(h)], k[:, lanes_of(h)], (((1,), (1,)), ((), ())),
-            preferred_element_type=F32,
-        ) * scaling
-        spacing = column(h, length) - runt[pl.ds(h, 1), :]
-        decay = jnp.where(wide >= tall, jnp.exp(jnp.minimum(spacing, 0.0)), 0.0)
+        grown, across_row = column(h), runt[pl.ds(h, 1), :]
+        strips = []
+        for first in range(0, length, size):
+            keys = k[pl.ds(first, size), lanes_of(h)]
+            weights = lax.dot_general(
+                q[pl.ds(first, length - first), lanes_of(h)], keys, (((1,), (1,)), ((), ())),
+                preferred_element_type=F32,
+            ) * scaling
+            spacing = grown[first:] - across_row[:, first:first + size]
+            strip = weights * jnp.exp(jnp.minimum(spacing, 0.0))
+            corner = lax.broadcasted_iota(jnp.int32, (size, size), 0) >= (
+                lax.broadcasted_iota(jnp.int32, (size, size), 1)
+            )
+            strip = [jnp.where(corner, strip[:size], 0.0).astype(BF16), strip[size:].astype(BF16)]
+            if first:
+                strip.insert(0, jnp.zeros((first, size), BF16))
+            strips.append(jnp.concatenate([p for p in strip if p.shape[0]], axis=0))
         att[:, lanes_of(h)] = jnp.dot(
-            (weights * decay).astype(BF16), v[:, lanes_of(h)], preferred_element_type=F32
+            jnp.concatenate(strips, axis=1), v[:, lanes_of(h)], preferred_element_type=F32
         )
 
     pl.loop(0, heads)(attend)
@@ -268,7 +306,7 @@
 
     @pl.loop(0, heads)
     def _(h):
-        grown = jnp.exp(column(h, size)) * scaling
+        grown = jnp.exp(column(h)) * scaling
         scaled = (q[:, lanes_of(h)].astype(F32) * grown).astype(BF16)
         whole = att[:, lanes_of(h)] + jnp.dot(scaled, incoming[h], preferred_element_type=F32)
         mean = jnp.mean(whole * whole, axis=1, keepdims=True)
@@ -308,8 +346,6 @@
         across[4].wait()
         across[5].wait()
         project(6, False)
-        for copy in first + second + onward:
-            copy.wait_send()
     else:
         for i, copy in enumerate(first):
             copy.wait()
@@ -319,6 +355,11 @@
             across[i].wait()
             project(offset, False)
 
+    if square:
+        for copy in first + second + onward:
+            copy.wait_send()
+    res, mix = q, k
+    loads[6].wait()
     step = 64
 
     @pl.loop(0, length // step)
@@ -330,39 +371,35 @@
         mean = jnp.mean(kept * kept, axis=1, keepdims=True)
         mix[at, :] = (kept * lax.rsqrt(mean + 1e-06) * gain[...]).astype(BF16)
 
-
-def expert_kernel(
-    n, slots,
-    mix, res, tok_col, tok_row, route, gate_h, up_h, down_h,
-    out,
-    gate, up, down, picked, arrived, hidden, produced, returned,
-    load_sem, a_send, a_recv, b_send, b_recv,
-):
-    me = lax.axis_index("seq")
-    length, width = mix.shape
     inner = gate.shape[1]
-    loads = [
-        pltpu.make_async_copy(src, dst, load_sem.at[i])
-        for i, (src, dst) in enumerate(((gate_h, gate), (up_h, up), (down_h, down)))
-    ]
-    for copy in loads:
-        copy.start()
-    greet(n, me)
+    picked = weight.at[pl.ds(0, n * slots)]
+    produced = weight.at[pl.ds(n * slots, n * slots)]
 
     def block(first, count=1):
         return pl.ds(first * slots, count * slots)
 
     def pick(first, count, into):
         lines = block(first, count)
-        places = lax.broadcasted_iota(jnp.int32, (count * slots, length), 1)
-        chosen = (tok_col[lines, :] == places).astype(F32).astype(BF16)
+        lanes = count * slots
+        row = flat(tok[...].astype(F32), first, count, -1.0)
+        column_of = jnp.broadcast_to(row, (size, lanes)).T
+        own_first = me * length
+        one_hot = jnp.concatenate([
+            jnp.where(
+                jnp.abs(
+                    column_of
+                    - (lax.broadcasted_iota(jnp.int32, (lanes, size), 1) + own_first + at).astype(F32)
+                ) < 0.5, 1.0, 0.0,
+            ).astype(BF16)
+            for at in range(0, length, size)
+        ], axis=1)
         tile = 512
 
         @pl.loop(0, width // tile)
         def _(i):
             cols = pl.ds(pl.multiple_of(i * tile, tile), tile)
             into[lines, cols] = jnp.dot(
-                chosen, mix[:, cols], preferred_element_type=F32
+                one_hot, mix[:, cols], preferred_element_type=F32
             ).astype(BF16)
 
     def out_copy(o):
@@ -404,6 +441,8 @@
 
     near = list(range(2, n - n // 4))
     far = list(range(n - n // 4, n))
+    loads[7].wait()
+    loads[8].wait()
     pick(2, len(near), picked)
     for o in near:
         out_copy(o).start()
@@ -411,7 +450,7 @@
     out_copy(1).start()
     pick(0, 1, arrived)
     pick(far[0], len(far), picked)
-    for copy in loads:
+    for copy in loads[9:]:
         copy.wait()
     out_copy(1).wait()
     expert(0, 2)
@@ -432,26 +471,38 @@
     for o in far:
         back_copy(o).start()
 
-    for o in range(1, n):
+    def mixing(first, count):
+        lanes = count * slots
+        token = flat(tok[...].astype(F32), first, count, -1.0)
+        share = flat(route[...], first, count, 0.0)
+        line = (lax.broadcasted_iota(jnp.int32, (length, lanes), 0) + me * length).astype(F32)
+        return jnp.where(jnp.abs(line - token) < 0.5, share, 0.0).astype(BF16)
+
+    tile = 512
+    early, late = mixing(0, far[0]), mixing(far[0], len(far))
+    for o in [1] + near:
         back_copy(o).wait()
-    lines = lax.broadcasted_iota(jnp.int32, (length, n * slots), 0)
-    mixing = jnp.where(tok_row[...] == lines, route[...], 0.0).astype(BF16)
-    tile = 512
 
     @pl.loop(0, width // tile)
     def _(i):
         cols = pl.ds(pl.multiple_of(i * tile, tile), tile)
-        gathered = jnp.dot(mixing, returned[:, cols], preferred_element_type=F32)
-        out[:, cols] = (res[:, cols].astype(F32) + gathered).astype(BF16)
-
-
-def by_offset(array, n, device):
-    axes = n.bit_length() - 1
-    cut = array.reshape((2,) * axes + array.shape[1:])
-    for axis in range(axes):
-        bit = (device // (n >> (axis + 1))) % 2
-        cut = jnp.where(bit == 1, jnp.flip(cut, axis), cut)
-    return cut.reshape(array.shape)
+        gathered = jnp.dot(
+            early, returned[block(0, far[0]), cols], preferred_element_type=F32
+        )
+        att[:, cols] = res[:, cols].astype(F32) + gathered
+
+    for o in far:
+        back_copy(o).wait()
+    writes = []
+    for i in range(width // tile):
+        cols = pl.ds(i * tile, tile)
+        att[:, cols] += jnp.dot(
+            late, returned[block(far[0], len(far)), cols], preferred_element_type=F32
+        )
+        writes.append(pltpu.make_async_copy(att.at[:, cols], out.at[:, cols], o_sem.at[i]))
+        writes[-1].start()
+    for copy in writes:
+        copy.wait()
 
 
 def shards(
@@ -466,21 +517,28 @@
     half = heads // 2
     bits = n.bit_length() - 2
     inner = gate_weight.shape[2]
-    vmem = pl.BlockSpec(memory_space=pltpu.VMEM)
-    anywhere = pl.BlockSpec(memory_space=pl.ANY)
+    hbm = pl.BlockSpec(memory_space=pltpu.HBM)
     dma = pltpu.SemaphoreType.DMA
-    rows_of = jax.ShapeDtypeStruct((length, width), BF16)
-
-    residual, mixed_in = pl.pallas_call(
-        functools.partial(attend_kernel, n, heads, size),
-        out_shape=(rows_of, rows_of),
-        in_specs=[anywhere] * 4 + [vmem] * 3 + [anywhere],
-        out_specs=(vmem, vmem),
+    chosen = token_index.shape[1]
+    slots = -(-chosen // 16) * 16
+
+    total = pl.pallas_call(
+        functools.partial(layer_kernel, n, heads, size, slots),
+        out_shape=jax.ShapeDtypeStruct((length, width), F32),
+        in_specs=[hbm] * 12,
+        out_specs=hbm,
         scratch_shapes=[
             pltpu.VMEM((length, width), BF16),
             pltpu.VMEM((length, width), BF16),
             pltpu.VMEM((length, width), BF16),
             pltpu.VMEM((length, width), BF16),
+            pltpu.VMEM((heads, length), F32),
+            pltpu.VMEM((1, width), F32),
+            pltpu.VMEM((n, chosen), jnp.int32),
+            pltpu.VMEM((n, chosen), F32),
+            pltpu.VMEM((width, inner), BF16),
+            pltpu.VMEM((width, inner), BF16),
+            pltpu.VMEM((inner, width), BF16),
             pltpu.VMEM((width, width), BF16),
             pltpu.VMEM((length, width), F32),
             pltpu.VMEM((length, width), BF16),
@@ -498,63 +556,35 @@
             pltpu.VMEM((heads, size, size), BF16),
             pltpu.VMEM((n, heads, size), F32),
             pltpu.VMEM((3, heads, size), F32),
-            dma((5,)),
+            pltpu.VMEM((n * slots, width), BF16),
+            pltpu.VMEM((n * slots, inner), BF16),
+            pltpu.VMEM((n * slots, width), BF16),
+            dma((12,)),
             dma((max(n, 13),)),
             dma((max(n, 13),)),
             dma((n,)),
             dma((n,)),
             dma((bits + 2,)),
             dma((bits + 2,)),
-        ],
-        compiler_params=pltpu.CompilerParams(
-            collective_id=0, has_side_effects=True, vmem_limit_bytes=48 * 2**20
-        ),
-        cost_estimate=pl.CostEstimate(
-            flops=2 * length * width * width, bytes_accessed=12 * length * width, transcendentals=0
-        ),
-        name="attend",
-    )(
-        queries, keys_in, values, stream, log_decay, log_decay.T, moe_gain[None, :], out_weight
-    )
-
-    chosen = token_index.shape[1]
-    slots = -(-chosen // 16) * 16
-    fill = ((0, 0), (0, slots - chosen))
-    places = jnp.pad(token_index - device * length, fill, constant_values=-1)
-    places = by_offset(places, n, device)
-    route = by_offset(jnp.pad(route_weight, fill), n, device).reshape(1, n * slots)
-
-    return pl.pallas_call(
-        functools.partial(expert_kernel, n, slots),
-        out_shape=rows_of,
-        in_specs=[vmem] * 5 + [anywhere] * 3,
-        out_specs=vmem,
-        scratch_shapes=[
-            pltpu.VMEM((width, inner), BF16),
-            pltpu.VMEM((width, inner), BF16),
-            pltpu.VMEM((inner, width), BF16),
-            pltpu.VMEM((n * slots, width), BF16),
-            pltpu.VMEM((n * slots, width), BF16),
-            pltpu.VMEM((n * slots, inner), BF16),
-            pltpu.VMEM((n * slots, width), BF16),
-            pltpu.VMEM((n * slots, width), BF16),
-            dma((3,)),
             dma((n,)),
             dma((n,)),
             dma((n,)),
             dma((n,)),
+            dma((width // 512,)),
         ],
         compiler_params=pltpu.CompilerParams(
-            collective_id=1, has_side_effects=True, vmem_limit_bytes=56 * 2**20
+            collective_id=0, has_side_effects=True, vmem_limit_bytes=62 * 2**20
         ),
         cost_estimate=pl.CostEstimate(
-            flops=6 * n * slots * width * inner, bytes_accessed=6 * width * inner, transcendentals=0
+            flops=2 * length * width * width + 6 * n * slots * width * inner,
+            bytes_accessed=6 * width * inner + 14 * length * width, transcendentals=0,
         ),
-        name="experts",
+        name="layer",
     )(
-        mixed_in, residual, places.reshape(n * slots, 1), places.reshape(1, n * slots), route,
-        gate_weight[0], up_weight[0], down_weight[0],
+        queries, keys_in, values, stream, log_decay.T, moe_gain[None, :], out_weight,
+        token_index, route_weight, gate_weight[0], up_weight[0], down_weight[0],
     )
+    return total.astype(BF16)
 
 
 def solution(mesh):

time: 154 us -> 134 us (0.87)
  local copies, waits for them, and re-layouts: 12.4 us -> 0 us
  Pallas kernels: 140 us -> 130 us
  other arithmetic: 1.49 us -> 3.27 us
    unnamed x14 -> x0, local copies, waits for them, and re-layouts: 9.94 us -> none
    pallas_call x2 -> x1, Pallas kernels: 140 us -> 130 us  [shards(): pl.pallas_call(functools.partial(layer_kernel, n, heads, size, slots), ou...]
    convert_element_type x0 -> x1, other arithmetic: none -> 3.27 us  [shards(): return total.astype(BF16)]
    another operation x3 -> x0, local copies, waits for them, and re-layouts: 2.37 us -> none  [the longest x1 1.02 us: shards(): places.reshape(n * slots, 1)]
where the time goes in v2:
time: 134 us
  Pallas kernels  130 us (97%)
  other arithmetic  3.27 us (2%)
    pallas_call x1, Pallas kernels, shards(): pl.pallas_call(functools.partial(layer_kernel, n, heads, size, slots), ou...  130 us
    convert_element_type x1, other arithmetic, shards(): return total.astype(BF16)  3.27 us

profile of v2, /device:TPU:1, one launch (start us, length us, event | category | flops | bytes accessed | tf_op | source)
XLA Modules:
  0.0 133.8 jit_solution(13849262482762407852)
XLA Ops:
  0.0 130.5 %layer.1 = f32[384,2048]{1,0:T(8,128)} custom-call(bf16[384,2048]{1,0:T(8,128)(2,1)} %q_h.1, bf16[384,2048]{1,0:T(8,128)(2,1)} %k_h.1, bf16[384,2048]{1,0:T(8,128)(2,1)} %v_h.1, bf16[384,2048]{1,0:T(8,128)(2,1)} %s_h.1, f32[16,384]{1,0:T(8,128)} %bitcast.8, f32[1,2048]{1,0:T(1,128)} %bitcast.9, bf16[256,2048]{1,0:T(8,128)(2,1)} %w_h.1, s32[8,96]{1,0:T(8,128)} %tok_h.1, ...), custom_call_target="tpu_custom_call" | custom-call | flops 16508780544 | bytes 28311552 | tf_op jit(solution)/shard_map/layer/pallas_call | solution.py:525
  130.5 3.3 %convert_element_type.3 = bf16[384,2048]{1,0:T(8,128)(2,1)} convert(f32[384,2048]{1,0:T(8,128)} %layer.1) | non-fusion elementwise | flops 786432 | bytes 4718592 | tf_op jit(solution)/shard_map/convert_element_type | solution.py:587

commit v3 on v2

--- a/solution.py
+++ b/solution.py
@@ -28,13 +28,15 @@
     )
 
 
-def greet(n, me):
+def greet(n, me, plane=None):
     barrier = pltpu.get_barrier_semaphore()
     for offset in range(1, n):
         pl.semaphore_signal(
             barrier, inc=1, device_id={"seq": flipped(me, offset)}, device_id_type=MESH
         )
-    pl.semaphore_wait(barrier, n - 1)
+    if plane is not None:
+        pl.semaphore_signal(barrier, inc=1, device_id={"dp": plane}, device_id_type=MESH)
+    pl.semaphore_wait(barrier, n - 1 if plane is None else n)
 
 
 def layer_kernel(
@@ -55,7 +57,6 @@
     length, width = q.shape
     rows = w_h.shape[0]
     half = heads // 2
-    low = rows // 2
     bits = n.bit_length() - 2
     scaling = size ** (-0.5)
 
@@ -68,51 +69,85 @@
             (gate_h, gate), (up_h, up), (down_h, down),
         ))
     ]
-    for i in (5, 0, 1, 2, 4, 3, 6, 7, 8):
+    for i in (4, 5, 0, 1, 2, 3, 6, 7, 8):
         loads[i].start()
-    greet(n, me)
-
-    def part(offset, piece):
-        start = flipped(me, offset) * rows
-        if piece == 0:
-            return pl.ds(pl.multiple_of(start, low), low)
-        if piece == 1:
-            return pl.ds(pl.multiple_of(start + low, low), low)
-        return pl.ds(pl.multiple_of(start, rows), rows)
-
-    def own(piece):
-        return w_h.at[pl.ds(piece * low, low)] if piece < 2 else w_h
-
-    def spread(slot, src, where, offset):
-        return remote(src, weight.at[where], w_send.at[slot], w_recv.at[slot], flipped(me, offset))
-
-    square = n == 8
+    square = n == 8 and lax.axis_size("dp") % 2 == 0
+    plane = flipped(lax.axis_index("dp"), 1)
+    odd = lax.axis_index("dp") % 2
+    greet(n, me, plane if square else None)
+
+    pieces = 8
+    some = rows // pieces
+
+    def strip(device, piece=None):
+        if piece is None:
+            return pl.ds(pl.multiple_of(device * rows, rows), rows)
+        return pl.ds(pl.multiple_of(device * rows + piece * some, some), some)
+
+    def spread(slot, where, axis, peer):
+        return pltpu.make_async_remote_copy(
+            src_ref=weight.at[where], dst_ref=weight.at[where],
+            send_sem=w_send.at[slot], recv_sem=w_recv.at[slot],
+            device_id={axis: peer}, device_id_type=MESH,
+        )
+
     if square:
-        first = [
-            spread(0, own(0), part(0, 0), 2),
-            spread(1, own(1), part(0, 1), 4),
+        beside = flipped(me, 4)
+        sent_x = me + odd * (beside - me)
+        from_x = flipped(sent_x, 2)
+        from_z = flipped(from_x, 4)
+        along_y = [spread(i, strip(me, i), "seq", beside) for i in range(pieces)]
+        along_x = [
+            spread(pieces + i, strip(sent_x, i), "seq", flipped(me, 2)) for i in range(pieces)
         ]
-        second = [
-            spread(2, own(1), part(0, 1), 2),
-            spread(3, own(0), part(0, 0), 4),
-        ]
-        onward = [
-            spread(4, weight.at[part(2, 0)], part(2, 0), 4),
-            spread(5, weight.at[part(4, 1)], part(4, 1), 2),
-        ]
-        across_own = [spread(6, own(2), part(0, 2), 1)]
-        across = [
-            spread(7 + i, weight.at[part(o, p)], part(o, p), 1)
-            for i, (o, p) in enumerate(((2, 0), (4, 1), (2, 1), (4, 0), (6, 0), (6, 1)))
+        along_z = [spread(2 * pieces + i, strip(from_x, i), "dp", plane) for i in range(pieces)]
+        share_own = spread(6 * pieces, strip(me), "seq", mate)
+        share_y, share_x, share_z = [
+            [spread((3 + j) * pieces + i, strip(kind, i), "seq", mate) for i in range(pieces)]
+            for j, kind in enumerate((beside, from_x, from_z))
         ]
     else:
         others = range(2, n, 2)
-        first = [spread(o, own(2), part(0, 2), o) for o in others]
-        second, onward = [], []
-        across_own = [spread(1, own(2), part(0, 2), 1)]
-        across = [spread(o + 1, weight.at[part(o, 2)], part(o, 2), 1) for o in others]
-    for copy in first + across_own:
-        copy.start()
+        direct = [spread(o, strip(me), "seq", flipped(me, o)) for o in others]
+        share_own = spread(1, strip(me), "seq", mate)
+        share = [spread(o + 1, strip(flipped(me, o)), "seq", mate) for o in others]
+
+    def begin(first, last):
+        if not square:
+            return
+        for i in range(first, last):
+            along_y[i].start()
+
+        @pl.when(odd == 0)
+        def _():
+            for i in range(first, last):
+                along_x[i].start()
+
+    def relay(turn):
+        if not square:
+            return
+        if turn < pieces:
+            along_y[turn].wait_recv()
+
+            @pl.when(odd == 1)
+            def _():
+                along_x[turn].start()
+
+            share_y[turn].start()
+        if 0 <= turn - 1 < pieces:
+            along_x[turn - 1].wait_recv()
+            along_z[turn - 1].start()
+            share_x[turn - 1].start()
+        if 0 <= turn - 2 < pieces:
+            along_z[turn - 2].wait_recv()
+            share_z[turn - 2].start()
+
+    loads[4].wait()
+    begin(0, 3)
+    share_own.start()
+    if not square:
+        for copy in direct:
+            copy.start()
 
     wide = lax.broadcasted_iota(jnp.int32, (length, length), 0)
     tall = lax.broadcasted_iota(jnp.int32, (length, length), 1)
@@ -209,7 +244,8 @@
                 exchange(b).start()
 
     send_state(0)
-    for copy in second + loads[9:]:
+    begin(3, pieces)
+    for copy in loads[9:]:
         copy.start()
     loads[2].wait()
 
@@ -235,7 +271,11 @@
             jnp.concatenate(strips, axis=1), v[:, lanes_of(h)], preferred_element_type=F32
         )
 
-    pl.loop(0, heads)(attend)
+    quarter = heads // 4
+    pl.loop(0, quarter)(attend)
+    relay(0)
+    pl.loop(quarter, 2 * quarter)(attend)
+    relay(1)
 
     group, ahead = first_end + last_end, jnp.zeros_like(first_end)
     for b in range(bits):
@@ -281,13 +321,12 @@
             send_state(b + 1)
         ahead = ahead + jnp.where(bit == 1, other, 0.0)
         group = group + other
-        if b == 0 and square:
-            first[0].wait_recv()
-            onward[0].start()
-            across[0].start()
-            first[1].wait_recv()
-            onward[1].start()
-            across[1].start()
+        if b == 0:
+            relay(2)
+            pl.loop(2 * quarter, 3 * quarter)(attend)
+            relay(3)
+            pl.loop(3 * quarter, heads)(attend)
+            relay(4)
 
     before_low[...] = before[...].astype(BF16)
     trade = remote(before_low, before_mate, s_send.at[bits + 1], s_recv.at[bits + 1], mate)
@@ -304,19 +343,21 @@
             mate_part = jnp.where(core == 1, state_mate[h].astype(F32), 0.0)
             incoming[h] = (earlier * coef[0, pl.ds(h, 1), :] + mate_part).astype(BF16)
 
-    @pl.loop(0, heads)
-    def _(h):
+    def finish(h):
         grown = jnp.exp(column(h)) * scaling
         scaled = (q[:, lanes_of(h)].astype(F32) * grown).astype(BF16)
         whole = att[:, lanes_of(h)] + jnp.dot(scaled, incoming[h], preferred_element_type=F32)
         mean = jnp.mean(whole * whole, axis=1, keepdims=True)
         normed[:, lanes_of(h)] = (whole * lax.rsqrt(mean + 1e-06)).astype(BF16)
 
+    pl.loop(0, heads // 2)(finish)
+    relay(5)
+    pl.loop(heads // 2, heads)(finish)
+    relay(6)
     tile = 512
 
-    def project(offset, fresh):
-        start = (flipped(me, offset) // 2) * (2 * rows)
-        inner = pl.ds(pl.multiple_of(start, 2 * rows), 2 * rows)
+    def project(device, fresh=False):
+        inner = pl.ds(pl.multiple_of((device // 2) * (2 * rows), 2 * rows), 2 * rows)
 
         @pl.loop(0, width // tile)
         def _(i):
@@ -324,40 +365,32 @@
             term = jnp.dot(normed[:, inner], weight[inner, cols], preferred_element_type=F32)
             att[:, cols] = term if fresh else att[:, cols] + term
 
-    loads[4].wait()
-    across_own[0].wait()
-    project(0, True)
+    share_own.wait()
+    project(me, True)
     if square:
-        second[0].wait_recv()
-        across[2].start()
-        second[1].wait_recv()
-        across[3].start()
-        across[0].wait()
-        across[2].wait()
-        project(2, False)
-        across[1].wait()
-        across[3].wait()
-        project(4, False)
-        onward[0].wait_recv()
-        across[4].start()
-        onward[1].wait_recv()
-        across[5].start()
+        relay(pieces - 1)
+        for copy in share_y:
+            copy.wait()
+        project(beside)
+        relay(pieces)
+        for copy in share_x:
+            copy.wait()
+        project(from_x)
+        relay(pieces + 1)
         loads[3].wait()
-        across[4].wait()
-        across[5].wait()
-        project(6, False)
+        for copy in share_z:
+            copy.wait()
+        project(from_z)
+        for copy in along_y + along_x + along_z:
+            copy.wait_send()
     else:
-        for i, copy in enumerate(first):
+        for i, copy in enumerate(direct):
             copy.wait()
-            across[i].start()
+            share[i].start()
         loads[3].wait()
-        for i, offset in enumerate(range(2, n, 2)):
-            across[i].wait()
-            project(offset, False)
-
-    if square:
-        for copy in first + second + onward:
-            copy.wait_send()
+        for i, o in enumerate(range(2, n, 2)):
+            share[i].wait()
+            project(flipped(me, o))
     res, mix = q, k
     loads[6].wait()
     step = 64
@@ -496,10 +529,11 @@
     writes = []
     for i in range(width // tile):
         cols = pl.ds(i * tile, tile)
-        att[:, cols] += jnp.dot(
+        gathered = jnp.dot(
             late, returned[block(far[0], len(far)), cols], preferred_element_type=F32
         )
-        writes.append(pltpu.make_async_copy(att.at[:, cols], out.at[:, cols], o_sem.at[i]))
+        v[:, cols] = (att[:, cols] + gathered).astype(BF16)
+        writes.append(pltpu.make_async_copy(v.at[:, cols], out.at[:, cols], o_sem.at[i]))
         writes[-1].start()
     for copy in writes:
         copy.wait()
@@ -522,9 +556,9 @@
     chosen = token_index.shape[1]
     slots = -(-chosen // 16) * 16
 
-    total = pl.pallas_call(
+    return pl.pallas_call(
         functools.partial(layer_kernel, n, heads, size, slots),
-        out_shape=jax.ShapeDtypeStruct((length, width), F32),
+        out_shape=jax.ShapeDtypeStruct((length, width), BF16),
         in_specs=[hbm] * 12,
         out_specs=hbm,
         scratch_shapes=[
@@ -560,8 +594,8 @@
             pltpu.VMEM((n * slots, inner), BF16),
             pltpu.VMEM((n * slots, width), BF16),
             dma((12,)),
-            dma((max(n, 13),)),
-            dma((max(n, 13),)),
+            dma((max(n, 49),)),
+            dma((max(n, 49),)),
             dma((n,)),
             dma((n,)),
             dma((bits + 2,)),
@@ -584,7 +618,6 @@
         queries, keys_in, values, stream, log_decay.T, moe_gain[None, :], out_weight,
         token_index, route_weight, gate_weight[0], up_weight[0], down_weight[0],
     )
-    return total.astype(BF16)
 
 
 def solution(mesh):

time: 134 us -> 138 us (1.030)
  Pallas kernels: 130 us -> 135 us
  other arithmetic: 3.27 us -> 0 us
  local copies, waits for them, and re-layouts: 0 us -> 2.73 us
    pallas_call x1, Pallas kernels: 130 us -> 135 us  [shards(): pl.pallas_call(functools.partial(layer_kernel, n, heads, size, slots), ou...]
    convert_element_type x1 -> x0, other arithmetic: 3.27 us -> none  [shards(): return total.astype(BF16)]
    unnamed x0 -> x1, local copies, waits for them, and re-layouts: none -> 2.73 us
where the time goes in v3:
time: 138 us; the launch traced here: 137 us
  Pallas kernels  135 us (98%)
  local copies, waits for them, and re-layouts  2.73 us (2%)
    pallas_call x1, Pallas kernels, shards(): pl.pallas_call(functools.partial(layer_kernel, n, heads, size, slots), ou...  135 us

profile of v3, /device:TPU:1, one launch (start us, length us, event | category | flops | bytes accessed | tf_op | source)
XLA Modules:
  0.0 137.4 jit_solution(17320823138114038212)
XLA Ops:
  0.0 134.7 %layer.1 = bf16[384,2048]{1,0:T(8,128)(2,1)} custom-call(bf16[384,2048]{1,0:T(8,128)(2,1)} %q_h.1, bf16[384,2048]{1,0:T(8,128)(2,1)} %k_h.1, bf16[384,2048]{1,0:T(8,128)(2,1)} %v_h.1, bf16[384,2048]{1,0:T(8,128)(2,1)} %s_h.1, f32[16,384]{1,0:T(8,128)} %bitcast.8, f32[1,2048]{1,0:T(1,128)} %bitcast.9, bf16[256,2048]{1,0:T(8,128)(2,1)} %w_h.1, s32[8,96]{1,0:T(8,128)} %tok_h.1, ...), custom_call_target="tpu_custom_call" | custom-call | flops 16508780544 | bytes 28311552 | tf_op jit(solution)/shard_map/layer/pallas_call | solution.py:559
  134.7 2.7 %copy.14 = bf16[384,2048]{1,0:T(8,128)(2,1)} copy(bf16[384,2048]{1,0:T(8,128)(2,1)} %layer.1) | data formatting | bytes 3145728

commit v4 on v2

--- a/solution.py
+++ b/solution.py
@@ -161,7 +161,7 @@
     loads[0].wait()
     loads[1].wait()
 
-    @pl.loop(0, heads)
+    @pl.loop(0, heads, unroll=4)
     def _(h):
         shrink = jnp.exp(ends[me, pl.ds(h, 1), :] - column(h))
         scaled = (k[:, lanes_of(h)].astype(F32) * shrink).astype(BF16)
@@ -235,7 +235,7 @@
             jnp.concatenate(strips, axis=1), v[:, lanes_of(h)], preferred_element_type=F32
         )
 
-    pl.loop(0, heads)(attend)
+    pl.loop(0, heads, unroll=2)(attend)
 
     group, ahead = first_end + last_end, jnp.zeros_like(first_end)
     for b in range(bits):
@@ -304,7 +304,7 @@
             mate_part = jnp.where(core == 1, state_mate[h].astype(F32), 0.0)
             incoming[h] = (earlier * coef[0, pl.ds(h, 1), :] + mate_part).astype(BF16)
 
-    @pl.loop(0, heads)
+    @pl.loop(0, heads, unroll=4)
     def _(h):
         grown = jnp.exp(column(h)) * scaling
         scaled = (q[:, lanes_of(h)].astype(F32) * grown).astype(BF16)
@@ -496,10 +496,11 @@
     writes = []
     for i in range(width // tile):
         cols = pl.ds(i * tile, tile)
-        att[:, cols] += jnp.dot(
+        gathered = jnp.dot(
             late, returned[block(far[0], len(far)), cols], preferred_element_type=F32
         )
-        writes.append(pltpu.make_async_copy(att.at[:, cols], out.at[:, cols], o_sem.at[i]))
+        v[:, cols] = (att[:, cols] + gathered).astype(BF16)
+        writes.append(pltpu.make_async_copy(v.at[:, cols], out.at[:, cols], o_sem.at[i]))
         writes[-1].start()
     for copy in writes:
         copy.wait()
@@ -522,9 +523,9 @@
     chosen = token_index.shape[1]
     slots = -(-chosen // 16) * 16
 
-    total = pl.pallas_call(
+    return pl.pallas_call(
         functools.partial(layer_kernel, n, heads, size, slots),
-        out_shape=jax.ShapeDtypeStruct((length, width), F32),
+        out_shape=jax.ShapeDtypeStruct((length, width), BF16),
         in_specs=[hbm] * 12,
         out_specs=hbm,
         scratch_shapes=[
@@ -584,7 +585,6 @@
         queries, keys_in, values, stream, log_decay.T, moe_gain[None, :], out_weight,
         token_index, route_weight, gate_weight[0], up_weight[0], down_weight[0],
     )
-    return total.astype(BF16)
 
 
 def solution(mesh):

time: 134 us -> 130 us (0.970)
  other arithmetic: 3.27 us -> 0 us
  Pallas kernels: 130 us -> 127 us
  local copies, waits for them, and re-layouts: 0 us -> 2.73 us
    convert_element_type x1 -> x0, other arithmetic: 3.27 us -> none  [shards(): return total.astype(BF16)]
    pallas_call x1, Pallas kernels: 130 us -> 127 us  [shards(): pl.pallas_call(functools.partial(layer_kernel, n, heads, size, slots), ou...]
    unnamed x0 -> x1, local copies, waits for them, and re-layouts: none -> 2.73 us
where the time goes in v4:
time: 130 us
  Pallas kernels  127 us (98%)
  local copies, waits for them, and re-layouts  2.73 us (2%)
    pallas_call x1, Pallas kernels, shards(): pl.pallas_call(functools.partial(layer_kernel, n, heads, size, slots), ou...  127 us
    unnamed x1, local copies, waits for them, and re-layouts  2.73 us

profile of v4, /device:TPU:1, one launch (start us, length us, event | category | flops | bytes accessed | tf_op | source)
XLA Modules:
  0.0 130.1 jit_solution(12268373545916301110)
XLA Ops:
  0.0 127.4 %layer.1 = bf16[384,2048]{1,0:T(8,128)(2,1)} custom-call(bf16[384,2048]{1,0:T(8,128)(2,1)} %q_h.1, bf16[384,2048]{1,0:T(8,128)(2,1)} %k_h.1, bf16[384,2048]{1,0:T(8,128)(2,1)} %v_h.1, bf16[384,2048]{1,0:T(8,128)(2,1)} %s_h.1, f32[16,384]{1,0:T(8,128)} %bitcast.8, f32[1,2048]{1,0:T(1,128)} %bitcast.9, bf16[256,2048]{1,0:T(8,128)(2,1)} %w_h.1, s32[8,96]{1,0:T(8,128)} %tok_h.1, ...), custom_call_target="tpu_custom_call" | custom-call | flops 16508780544 | bytes 28311552 | tf_op jit(solution)/shard_map/layer/pallas_call | solution.py:526
  127.4 2.7 %copy.14 = bf16[384,2048]{1,0:T(8,128)(2,1)} copy(bf16[384,2048]{1,0:T(8,128)(2,1)} %layer.1) | data formatting | bytes 3145728
